TPU v7x, 32 devices: a whole 2x2x4 slice. The times are simulated.
32 devices in a mesh: tiles: 8 (over z, core), chan: 4 (over y, x).
Axes of the slice: x: 2, y: 2, z: 4, core: 2. Of those that a mesh axis runs over, the one named last changes fastest.
Arguments:
- atmos_state: bfloat16 [64, 192, 256], P('tiles', 'chan'), may hold values from -6 to 6
- ocean_state: bfloat16 [64, 128, 256], P('tiles', 'chan'), may hold values from -6 to 6
- atmos_weight: bfloat16 [9, 192, 192], P(None, 'chan'), may hold values from -0.15625 to 0.15625
- ocean_weight: bfloat16 [9, 128, 128], P(None, 'chan'), may hold values from -0.1875 to 0.1875
- couple_weight: bfloat16 [128, 192], P('chan'), may hold values from -0.4375 to 0.4375
- sea_mask: int32 [64], replicated, may hold values from 0 to 1, as said below
- neighbours: int32 [64, 4], replicated, may hold values from 0 to 63, as said below
- rotations: int32 [64, 4], replicated, may hold values from 0 to 7
Outputs:
- atmos_next: bfloat16 [64, 192, 256], P('tiles', 'chan')
- ocean_next: bfloat16 [48, 128, 256], P('tiles', 'chan')
Inputs may be any that keep to these rules, and one draw needn't show every extreme that they name: `sea_mask`: exactly 48 of the 64 entries are 1; the tiles of blocks 2k and 2k + 1 of 8 tiles hold exactly 12 sea tiles together, and each such block holds between 4 and 8. neighbours[t, s] lies in the block of 8 tiles that holds t, or in the block just before or just after it, cyclically over the 8 blocks.
All inputs are finite; a program needn't handle non-finite values.
Results may differ from a plain program's by a relative error of at most 0.0034.
Values may be sent and summed in bfloat16 or wider, within the bound.
A program may use at most 64 MiB of HBM per device.

v0:
```python
import jax
import jax.numpy as jnp
from jax import lax
from jax.sharding import PartitionSpec as P

SIDE = 16


def padded_2(cells, sides, width):
    for axis, dim in sides:
        count = lax.axis_size(axis)
        head = lax.slice_in_dim(cells, 0, width, axis=dim)
        tail = lax.slice_in_dim(cells, cells.shape[dim] - width, cells.shape[dim], axis=dim)
        cells = jnp.concatenate(
            [
                lax.ppermute(tail, axis, [(i, (i + 1) % count) for i in range(count)]),
                cells,
                lax.ppermute(head, axis, [((i + 1) % count, i) for i in range(count)]),
            ],
            axis=dim,
        )
    return cells


def partner(value, axis, distance):
    mask = 2**distance
    pairs = [(source, source ^ mask) for source in range(lax.axis_size(axis))]
    return lax.ppermute(value, axis, pairs)


def edge_set(tile_field):
    tile_count, chan_count = (tile_field.shape[0], tile_field.shape[1])
    tile_grid = tile_field.reshape(tile_count, chan_count, SIDE, SIDE)
    return jnp.stack(
        [
            tile_grid[:, :, 0, :],
            tile_grid[:, :, :, SIDE - 1],
            tile_grid[:, :, SIDE - 1, :],
            tile_grid[:, :, :, 0],
        ],
        axis=2,
    )


def pick_rims(edge_strips, adjacent, turn_codes):
    picked = edge_strips[adjacent]
    side_index = turn_codes % 4
    chosen = picked[:, :, :, 0, :]
    for edge_id in range(1, 4):
        chosen = jnp.where(
            (side_index == edge_id)[:, :, None, None], picked[:, :, :, edge_id, :], chosen
        )
    return jnp.where((turn_codes >= 4)[:, :, None, None], chosen[..., ::-1], chosen)


def pad_tile(tile_field, rim_cells):
    tile_count, chan_count = (tile_field.shape[0], tile_field.shape[1])
    tile_grid = tile_field.reshape(tile_count, chan_count, SIDE, SIDE)
    upper_row = jnp.pad(rim_cells[:, 0], ((0, 0), (0, 0), (1, 1)))[:, :, None, :]
    bottom = jnp.pad(rim_cells[:, 2], ((0, 0), (0, 0), (1, 1)))[:, :, None, :]
    middle = jnp.concatenate(
        [rim_cells[:, 3][:, :, :, None], tile_grid, rim_cells[:, 1][:, :, :, None]], axis=3
    )
    assembled = jnp.concatenate([upper_row, middle, bottom], axis=2).reshape(
        tile_count, chan_count, (SIDE + 2) * (SIDE + 2)
    )
    return jnp.pad(assembled, ((0, 0), (0, 0), (0, 2)))


def trim_columns(accum):
    tile_count, chan_count = (accum.shape[0], accum.shape[1])
    return accum.reshape(tile_count, chan_count, SIDE, SIDE + 2)[:, :, :, :SIDE].reshape(
        tile_count, chan_count, SIDE * SIDE
    )


def conv_step(weight, accum, piece):
    row_width = SIDE + 2
    out_span = SIDE * row_width
    for tap_index in range(9):
        offset = tap_index // 3 * row_width + tap_index % 3
        accum = accum + jnp.einsum(
            "oc,bcp->bop",
            weight[tap_index],
            piece[:, :, offset : offset + out_span],
            preferred_element_type=jnp.float32,
        )
    return accum


def ocean_layer(padded, forcing, own_state, ocean_weight, couple_weight):
    tile_count = padded.shape[0]
    out_chans = ocean_weight.shape[1]
    conv_start = jnp.zeros((tile_count, out_chans, SIDE * (SIDE + 2)), jnp.float32)
    conv_accum = conv_step(
        ocean_weight, conv_start, lax.all_gather(padded, "chan", axis=1, tiled=True)
    )
    couple_accum = jnp.einsum(
        "oc,bcp->bop",
        couple_weight,
        lax.all_gather(forcing, "chan", axis=1, tiled=True),
        preferred_element_type=jnp.float32,
    )
    mixed = trim_columns(conv_accum) + couple_accum
    return (own_state.astype(jnp.float32) + jax.nn.gelu(mixed, approximate=True)).astype(
        jnp.bfloat16
    )


def local(
    atmos_state,
    ocean_state,
    atmos_weight,
    ocean_weight,
    couple_weight,
    sea_mask,
    neighbours,
    rotations,
):
    per_dev = atmos_state.shape[0]
    atmos_local = atmos_state.shape[1]
    ocean_local = ocean_state.shape[1]
    groups = lax.axis_size("tiles")
    tile_group = lax.axis_index("tiles")
    first_tile = tile_group * per_dev
    sea_here = lax.dynamic_slice_in_dim(sea_mask, first_tile, per_dev, 0)
    sea_field = ocean_state * sea_here.astype(jnp.bfloat16)[:, None, None]
    edge_strips = jnp.concatenate([edge_set(atmos_state), edge_set(sea_field)], axis=1)
    widened = padded_2(edge_strips.reshape(per_dev, -1), (("tiles", 0),), per_dev)
    widened = widened.reshape(3 * per_dev, atmos_local + ocean_local, 4, SIDE)
    adjacent = lax.dynamic_slice_in_dim(neighbours, first_tile, per_dev, 0)
    turn_codes = lax.dynamic_slice_in_dim(rotations, first_tile, per_dev, 0)
    local_adjacent = (adjacent // per_dev - tile_group + 1) % groups * per_dev + adjacent % per_dev
    rim_cells = pick_rims(widened, local_adjacent, turn_codes)
    atmos_pad = pad_tile(atmos_state, rim_cells[:, :, :atmos_local])
    atmos_start = jnp.zeros((per_dev, atmos_weight.shape[1], SIDE * (SIDE + 2)), jnp.float32)
    atmos_accum = conv_step(
        atmos_weight, atmos_start, lax.all_gather(atmos_pad, "chan", axis=1, tiled=True)
    )
    atmos_next = (
        atmos_state.astype(jnp.float32) + jax.nn.gelu(trim_columns(atmos_accum), approximate=True)
    ).astype(jnp.bfloat16)
    per_owner = per_dev * 3 // 4
    ocean_total = per_owner * groups
    counts = jnp.sum(sea_mask.reshape(groups, per_dev), axis=1)
    starts = jnp.cumsum(counts) - counts
    sea_rank = jnp.cumsum(sea_mask) - 1
    rank_spots = jnp.where(sea_mask == 1, sea_rank, ocean_total)
    tile_of_rank = (
        jnp.zeros((ocean_total,), jnp.int32)
        .at[rank_spots]
        .set(jnp.arange(sea_mask.shape[0], dtype=jnp.int32), mode="drop")
    )
    my_first = starts[tile_group]
    my_last = my_first + counts[tile_group]
    parity = tile_group % 2
    pair_base = tile_group // 2 * 2 * per_owner
    slot_ids = jnp.arange(per_owner, dtype=jnp.int32)
    ranks_send = pair_base + 2 * slot_ids + (1 - parity)
    ranks_own = pair_base + 2 * slot_ids + parity
    send_tile = jnp.clip(tile_of_rank[ranks_send] - first_tile, 0, per_dev - 1)
    own_tile = jnp.clip(tile_of_rank[ranks_own] - first_tile, 0, per_dev - 1)
    from_here = (ranks_own >= my_first) & (ranks_own < my_last)
    block_width = (ocean_local + atmos_local) * SIDE * SIDE
    sea_block = jnp.concatenate([ocean_state, atmos_next], axis=1).reshape(per_dev, block_width)
    rim_flat = rim_cells[:, :, atmos_local:].reshape(per_dev, -1)
    packed = jnp.concatenate([sea_block, rim_flat], axis=1)
    received = partner(packed[send_tile], "tiles", 0)
    own_packed = jnp.where(from_here[:, None], packed[own_tile], received)
    own_block = own_packed[:, :block_width].reshape(
        per_owner, ocean_local + atmos_local, SIDE * SIDE
    )
    own_rims = own_packed[:, block_width:].reshape(per_owner, 4, ocean_local, SIDE)
    own_state = own_block[:, :ocean_local]
    ocean_next = ocean_layer(
        pad_tile(own_state, own_rims),
        own_block[:, ocean_local:],
        own_state,
        ocean_weight,
        couple_weight,
    )
    return (atmos_next, ocean_next)


def solution(mesh):
    placed = (
        P("tiles", "chan", None),
        P("tiles", "chan", None),
        P(None, "chan", None),
        P(None, "chan", None),
        P("chan", None),
        P(),
        P(),
        P(),
    )
    return jax.shard_map(
        local,
        mesh=mesh,
        in_specs=placed,
        out_specs=(P("tiles", "chan", None), P("tiles", "chan", None)),
        check_vma=False,
    )
```

profile of v0, /device:TPU:0, one launch (start us, length us, event | category | flops | bytes accessed | tf_op | source)
XLA Modules:
  0.0 75.4 jit_solution(4838516931697906676)
XLA Ops:
  0.7 1.2 %copy.64 = bf16[8,48,256]{1,2,0:T(8,128)(2,1)S(1)} copy(bf16[8,48,256]{2,1,0:T(8,128)(2,1)} %param.8) | data formatting | bytes 393216 | tf_op args[0]
  2.9 0.4 copy.70
  3.2 0.9 %reshape.202 = bf16[8,5120]{1,0:T(8,128)(2,1)S(1)} reshape(bf16[8,80,4,16]{3,2,1,0:T(4,128)(2,1)S(1)} %copy.70) | data formatting | bytes 163840 | tf_op jit(solution)/shard_map/reshape | solution.py:129
  4.2 4.5 %collective-permute-start.1 = (bf16[8,5120]{1,0:T(8,128)(2,1)S(1)}, bf16[8,5120]{1,0:T(8,128)(2,1)S(1)}, u32[]{:S(2)}, u32[]{:S(2)}) collective-permute-start(bf16[8,5120]{1,0:T(8,128)(2,1)S(1)} %reshape.202), channel_id=1, source_target_pairs={{4,0},{8,4},{12,8},{16,12},{20,16},{24,20},{28,24},{0,28},{5,1},{9... | collective-permute-start | bytes 245768 | tf_op jit(solution)/shard_map/ppermute | solution.py:18
  9.8 0.8 %scatter_custom_fusion = s32[48]{0:T(128)S(1)} fusion(s32[64]{0:T(128)S(1)} %compare_select_fusion.5, s32[64]{0:T(128)S(1)} %iota.13, s32[]{:T(128)} %constant.101.clone.1), kind=kCustom, calls=%fused_computation.180 | custom fusion | bytes 196 | tf_op jit(solution)/shard_map/scatter | solution.py:152
  10.6 0.6 gather_fusion.3
  11.3 0.6 gather_fusion.1
  11.9 2.4 %collective-permute-done = bf16[8,5120]{1,0:T(8,128)(2,1)S(1)} collective-permute-done((bf16[8,5120]{1,0:T(8,128)(2,1)S(1)}, bf16[8,5120]{1,0:T(8,128)(2,1)S(1)}, u32[]{:S(2)}, u32[]{:S(2)}) %collective-permute-start) | collective-permute-done | bytes 81952 | tf_op jit(solution)/shard_map/ppermute | solution.py:16
  14.4 0.5 concatenate.30
  14.9 0.3 copy.71
  15.2 0.5 concatenate.31
  15.7 0.3 copy.72
  16.1 0.6 gather_fusion
  17.7 0.3 reshape.210
  18.0 0.5 pad_maximum_fusion
  18.6 0.5 copy.83
  19.2 15.2 %all_gather.9 = bf16[8,192,326]{2,1,0:T(8,128)(2,1)S(1)} all-gather(bf16[8,48,326]{2,1,0:T(8,128)(2,1)S(1)} %pad.24), channel_id=1, replica_groups=mesh['tiles'=8,'chan'=4] {'chan'}, dimensions={1}, use_global_device_ids=true | all-gather | bytes 1251840 | tf_op jit(solution)/shard_map/all_gather | solution.py:138
  34.4 0.3 fusion.9
  34.7 0.5 convolution_add_fusion.7
  35.3 0.5 convolution_add_fusion.6
  35.8 0.5 convolution_add_fusion.5
  36.3 0.5 convolution_add_fusion.4
  36.9 0.5 convolution_add_fusion.3
  37.4 0.5 convolution_add_fusion.2
  37.9 0.5 convolution_add_fusion.1
  38.4 0.5 fusion
  39.0 0.5 copy.84
  39.8 0.4 fusion.21
  40.8 0.7 gather_fusion.4
  41.6 0.6 dynamic_slice.19
  42.2 0.6 dynamic_slice.18
  44.1 0.7 compare_and_fusion
  44.8 0.9 %copy.109 = bf16[8,48,256]{2,1,0:T(8,128)(2,1)} copy(bf16[8,48,256]{1,2,0:T(8,128)(2,1)S(1)} %fusion.21) | data formatting | bytes 393216
  45.7 0.7 gather_fusion.2
  47.7 0.4 pad_maximum_fusion.1
  48.6 10.6 %all_gather.10 = bf16[6,128,326]{2,1,0:T(8,128)(2,1)S(1)} all-gather(bf16[6,32,326]{2,1,0:T(8,128)(2,1)S(1)} %pad.27.clone), channel_id=1, replica_groups=mesh['tiles'=8,'chan'=4] {'chan'}, dimensions={1}, use_global_device_ids=true | all-gather | bytes 625920 | tf_op jit(solution)/shard_map/all_gather | solution.py:96
  59.4 0.4 convolution_add_fusion.15
  59.8 0.4 convolution_add_fusion.14
  60.2 0.4 convolution_add_fusion.13
  60.5 0.4 convolution_add_fusion.12
  60.9 0.4 convolution_add_fusion.11
  61.3 0.4 convolution_add_fusion.10
  61.7 0.4 convolution_add_fusion.9
  62.1 0.4 fusion.11
  62.4 10.3 %all_gather.11 = bf16[6,192,256]{2,1,0:T(8,128)(2,1)S(1)} all-gather(bf16[6,48,256]{2,1,0:T(8,128)(2,1)S(1)} %slice.311), channel_id=1, replica_groups=mesh['tiles'=8,'chan'=4] {'chan'}, dimensions={1}, use_global_device_ids=true | all-gather | bytes 737280 | tf_op jit(solution)/shard_map/all_gather | solution.py:101
  72.7 1.0 %reshape.216 = f32[6,32,16,18]{3,2,1,0:T(8,128)S(1)} reshape(f32[6,32,288]{2,1,0:T(8,128)S(1)} %fusion.11) | data formatting | bytes 442368 | tf_op jit(solution)/shard_map/reshape | solution.py:72
  73.7 0.6 copy.107
  74.5 0.9 %fusion.40 = bf16[6,32,256]{2,1,0:T(8,128)(2,1)} fusion(f32[6,32,256]{2,1,0:T(8,128)S(1)} %copy.108, bf16[6,192,256]{2,1,0:T(8,128)(2,1)S(1)} %all_gather.11, bf16[32,192]{1,0:T(8,128)(2,1)S(1)} %copy-done, bf16[6,80,256]{2,1,0:T(8,128)(2,1)S(1)} %bitcast.195), kind=kOutput, calls=%fused_computation.73 | convolution fusion | flops 19464192 | bytes 995328 | tf_op jit(solution)/shard_map/oc,bcp->bop/dot_general | solution.py:98
  (90 shorter events, 6.3 us)
Async XLA Ops:
  0.6 73.9 %copy-start = (bf16[32,192]{1,0:T(8,128)(2,1)S(1)}, bf16[32,192]{1,0:T(8,128)(2,1)}, u32[]{:S(2)}) copy-start(bf16[32,192]{1,0:T(8,128)(2,1)} %param.12) | copy-start | bytes 36868
  0.6 1.4 %copy-start.2 = (bf16[8,32,256]{2,1,0:T(8,128)(2,1)S(1)}, bf16[8,32,256]{2,1,0:T(8,128)(2,1)}, u32[]{:S(2)}) copy-start(bf16[8,32,256]{2,1,0:T(8,128)(2,1)} %param.9) | copy-start | bytes 393220
  0.7 1.7 %copy-start.4 = (s32[64]{0:T(128)S(1)}, s32[64]{0:T(128)}, u32[]{:S(2)}) copy-start(s32[64]{0:T(128)} %param.13) | copy-start | bytes 772
  2.7 6.1 %copy-start.5 = (s32[64,4]{0,1:T(4,128)S(1)}, s32[64,4]{0,1:T(4,128)}, u32[]{:S(2)}) copy-start(s32[64,4]{0,1:T(4,128)} %param.14) | copy-start | bytes 3076
  2.7 6.4 %copy-start.6 = (s32[64,4]{0,1:T(4,128)S(1)}, s32[64,4]{0,1:T(4,128)}, u32[]{:S(2)}) copy-start(s32[64,4]{0,1:T(4,128)} %param.15) | copy-start | bytes 3076
  4.2 11.0 %collective-permute-start.1 = (bf16[8,5120]{1,0:T(8,128)(2,1)S(1)}, bf16[8,5120]{1,0:T(8,128)(2,1)S(1)}, u32[]{:S(2)}, u32[]{:S(2)}) collective-permute-start(bf16[8,5120]{1,0:T(8,128)(2,1)S(1)} %reshape.202), channel_id=1, source_target_pairs={{4,0},{8,4},{12,8},{16,12},{20,16},{24,20},{28,24},{0,28},{5,1},{9... | collective-permute-start | bytes 245768 | tf_op jit(solution)/shard_map/ppermute | solution.py:18
  8.7 5.7 %collective-permute-start = (bf16[8,5120]{1,0:T(8,128)(2,1)S(1)}, bf16[8,5120]{1,0:T(8,128)(2,1)S(1)}, u32[]{:S(2)}, u32[]{:S(2)}) collective-permute-start(bf16[8,5120]{1,0:T(8,128)(2,1)S(1)} %reshape.202), channel_id=1, source_target_pairs={{0,4},{4,8},{8,12},{12,16},{16,20},{20,24},{24,28},{28,0},{1,5},{5... | collective-permute-start | bytes 245768 | tf_op jit(solution)/shard_map/ppermute | solution.py:16
  19.1 15.3 %copy-start.1 = (bf16[9,48,192]{2,1,0:T(8,128)(2,1)S(1)}, bf16[9,48,192]{2,1,0:T(8,128)(2,1)}, u32[]{:S(2)}) copy-start(bf16[9,48,192]{2,1,0:T(8,128)(2,1)} %param.10) | copy-start | bytes 497668
  41.6 4.8 %collective-permute-start.2 = (bf16[6,22528]{1,0:T(8,128)(2,1)S(1)}, bf16[6,22528]{1,0:T(8,128)(2,1)S(1)}, u32[]{:S(2)}, u32[]{:S(2)}) collective-permute-start(bf16[6,22528]{1,0:T(8,128)(2,1)S(1)} %gather_fusion.4), channel_id=1, source_target_pairs={{0,4},{4,0},{8,12},{12,8},{16,20},{20,16},{24,28},{28,24},{1,5},{5... | collective-permute-start | bytes 811016 | tf_op jit(solution)/shard_map/ppermute | solution.py:28
  48.1 11.1 %copy-start.3 = (bf16[9,32,128]{2,1,0:T(8,128)(2,1)S(1)}, bf16[9,32,128]{2,1,0:T(8,128)(2,1)}, u32[]{:S(2)}) copy-start(bf16[9,32,128]{2,1,0:T(8,128)(2,1)} %param.11) | copy-start | bytes 221188
where the time goes:
time: 75.7 us; the launch traced here: 75.4 us
  blocking collectives  36.1 us (48%)
  local copies, waits for them, and re-layouts  17.3 us (23%)
  matrix products  8.62 us (11%)
  starting transfers between devices  4.61 us (6%)
  other arithmetic  3.81 us (5%)
  between operations  2.63 us (3%)
  waiting for transfers between devices  2.42 us (3%)
    all_gather x1, blocking collectives, local(): lax.all_gather(atmos_pad, 'chan', axis=1, tiled=True)  15.2 us
    all_gather x1, blocking collectives, ocean_layer(): lax.all_gather(padded, 'chan', axis=1, tiled=True)  10.6 us
    all_gather x1, blocking collectives, ocean_layer(): lax.all_gather(forcing, 'chan', axis=1, tiled=True)  10.3 us
    dot_general x18, matrix products, conv_step(): jnp.einsum('oc,bcp->bop', weight[tap_index], piece[:, :, offset:offset +...  7.72 us
    ppermute x1, starting transfers between devices, padded_2(): lax.ppermute(head, axis, [((i + 1) % count, i) for i in range(count)])  4.53 us
    unnamed x21, local copies, waits for them, and re-layouts  2.74 us
    ppermute x1, waiting for transfers between devices, padded_2(): lax.ppermute(tail, axis, [(i, (i + 1) % count) for i in range(count)])  2.42 us
    concatenate x4, local copies, waits for them, and re-layouts, padded_2(): jnp.concatenate([lax.ppermute(tail, axis, [(i, (i + 1) % count) for i in...  1.6 us
  transfers between devices with their start and end apart: 3, of which 1 were waited for; matrix products, arithmetic and copies ran while one was open for 10% of the time, Pallas kernels for 0%

commit v1 on v0

--- a/solution.py
+++ b/solution.py
@@ -1,6 +1,11 @@
+import functools
+
 import jax
 import jax.numpy as jnp
+import numpy as np
 from jax import lax
+from jax.experimental import pallas as pl
+from jax.experimental.pallas import tpu as pltpu
 from jax.sharding import PartitionSpec as P
 
 SIDE = 16
@@ -182,7 +187,324 @@
     return (atmos_next, ocean_next)
 
 
+MESH = pl.DeviceIdType.MESH
+PIX = SIDE * SIDE
+BF = jnp.bfloat16
+F32 = jnp.float32
+
+
+def edge_matrix():
+    out = np.zeros((2, PIX, 128), np.float32)
+    for half in range(2):
+        for q in range(SIDE):
+            pixels = (q, q * SIDE + SIDE - 1, (SIDE - 1) * SIDE + q, q * SIDE)
+            for edge, pixel in enumerate(pixels):
+                out[half, pixel, half * 64 + edge * SIDE + q] = 1
+    return out
+
+
+def shift_matrix():
+    out = np.zeros((9, PIX + 128, PIX), np.float32)
+    for tap in range(9):
+        for i in range(SIDE):
+            for j in range(SIDE):
+                row, col = i + tap // 3 - 1, j + tap % 3 - 1
+                in_row, in_col = 0 <= row < SIDE, 0 <= col < SIDE
+                if in_row and in_col:
+                    out[tap, row * SIDE + col, i * SIDE + j] = 1
+                elif in_row or in_col:
+                    if in_col:
+                        place = (0 if row < 0 else 2) * SIDE + col
+                    else:
+                        place = (3 if col < 0 else 1) * SIDE + row
+                    for half in range(2):
+                        out[tap, PIX + half * 64 + place, i * SIDE + j] = 1
+    return out
+
+
+def gelu(v):
+    return 0.5 * v * (1.0 + jnp.tanh(np.float32(np.sqrt(2.0 / np.pi)) * (v + 0.044715 * (v * v * v))))
+
+
+def dot(x, y):
+    return jnp.dot(x, y, preferred_element_type=F32)
+
+
+def owner_kernel(
+    groups, nchan, at_hbm, oc_hbm, wa_hbm, wo_hbm, wc_hbm, mask_s, nbr_s, rot_s, ev_hbm, sh_hbm,
+    outa, outo,
+    at_v, oc_v, ev, sh, xx, ew, rl, rg, sel, wa, wo, wc, xs, an, on, og,
+    loc, ssem, rsem,
+):
+    per_dev, ach, _ = at_hbm.shape
+    och = oc_hbm.shape[1]
+    atot = ach * nchan
+    tp = per_dev // nchan
+    rows = ach + och
+    b = lax.axis_index("tiles")
+    c = lax.axis_index("chan")
+    par = lax.rem(b, 2)
+    sib = b + 1 - 2 * par
+    nxt = lax.rem(b + 1, groups)
+    prv = lax.rem(b + groups - 1, groups)
+    other = jnp.where(par == 0, prv, nxt)
+    half_o = och // 2
+
+    bar = pltpu.get_barrier_semaphore()
+    for d in range(nchan):
+        peer = lax.rem(c + d, nchan)
+        if d:
+            pl.semaphore_signal(bar, inc=1, device_id=(b, peer), device_id_type=MESH)
+        pl.semaphore_signal(bar, inc=1, device_id=(sib, peer), device_id_type=MESH)
+    pl.semaphore_signal(bar, inc=1, device_id=(other, c), device_id_type=MESH)
+
+    def arow(i):
+        return pl.ds(pl.multiple_of(i * ach, 16), ach)
+
+    def orow(i):
+        return pl.ds(pl.multiple_of(i * och, 16), och)
+
+    def xorow(i):
+        return pl.ds(pl.multiple_of(atot + i * och, 16), och)
+
+    def ohalf(i, k):
+        return pl.ds(pl.multiple_of(i * och + k * half_o, 16), half_o)
+
+    own = pl.ds(c * tp, tp)
+    locals_ = [
+        (at_hbm, at_v),
+        (oc_hbm, oc_v),
+        (ev_hbm, ev),
+        (at_hbm.at[own], xx.at[:, arow(c), :]),
+        (oc_hbm.at[own], xx.at[:, xorow(c), :]),
+        (sh_hbm, sh),
+        (wa_hbm, wa.at[:, arow(c), :]),
+        (wo_hbm, wo.at[:, orow(c), :]),
+        (wc_hbm, wc.at[orow(c), :]),
+    ]
+    lcopies = [pltpu.make_async_copy(s, t, loc.at[i]) for i, (s, t) in enumerate(locals_)]
+    for cp in lcopies:
+        cp.start()
+    for cp in lcopies[:3]:
+        cp.wait()
+
+    first = b * per_dev
+    lane128 = lax.broadcasted_iota(jnp.int32, (1, 128), 1)
+    for u in range(per_dev // 2):
+        at_e = dot(at_v[2 * u], ev[0]) + dot(at_v[2 * u + 1], ev[1])
+        oc_e = dot(oc_v[2 * u], ev[0]) + dot(oc_v[2 * u + 1], ev[1])
+        keep = jnp.where(lane128 < 64, mask_s[first + 2 * u], mask_s[first + 2 * u + 1])
+        ew[1, :ach, u * 128 : u * 128 + 128] = at_e.astype(BF)
+        ew[1, ach:, u * 128 : u * 128 + 128] = jnp.where(keep > 0, oc_e, 0.0).astype(BF)
+
+    counter = [0]
+
+    def remote(src, dst, dev):
+        i = counter[0]
+        counter[0] += 1
+        return pltpu.make_async_remote_copy(
+            src_ref=src, dst_ref=dst, send_sem=ssem.at[i], recv_sem=rsem.at[i],
+            device_id=dev, device_id_type=MESH,
+        )
+
+    pl.semaphore_wait(bar, 2 * nchan)
+    edges = [remote(ew.at[1], ew.at[0], (nxt, c)), remote(ew.at[1], ew.at[2], (prv, c))]
+    for cp in edges:
+        cp.start()
+    states, weights = [], []
+    for d in range(1, nchan):
+        peer = lax.rem(c + d, nchan)
+        theirs = pl.ds(peer * tp, tp)
+        states += [
+            remote(at_hbm.at[theirs], xx.at[:, arow(c), :], (b, peer)),
+            remote(oc_hbm.at[theirs], xx.at[:, xorow(c), :], (b, peer)),
+        ]
+    for cp in states:
+        cp.start()
+    for d in range(1, nchan):
+        peer = lax.rem(c + d, nchan)
+        taps = pl.ds(par * 4, 5)
+        hrow = pl.ds(pl.multiple_of(par * half_o, 16), half_o)
+        weights += [
+            remote(wa_hbm.at[taps], wa.at[taps, arow(c), :], (b, peer)),
+            remote(wo_hbm.at[:, hrow, :], wo.at[:, ohalf(c, par), :], (b, peer)),
+            remote(wc_hbm.at[hrow], wc.at[ohalf(c, par), :], (b, peer)),
+        ]
+    for cp in weights:
+        cp.start()
+
+    width = per_dev * 64
+    lane = lax.broadcasted_iota(jnp.int32, (1, width), 1)
+    strip, place = lane // SIDE, lane % SIDE
+    src = jnp.zeros((1, width), jnp.int32)
+    for t in range(per_dev):
+        for s in range(4):
+            nb = nbr_s[first + t, s]
+            rot = rot_s[first + t, s]
+            slot = lax.rem(lax.div(nb, per_dev) - b + 1 + groups, groups)
+            base = slot * width + lax.rem(nb, per_dev) * 64 + lax.rem(rot, 4) * SIDE
+            back = jnp.where(rot >= 4, SIDE - 1, 0)
+            step = jnp.where(rot >= 4, -1, 1)
+            src = jnp.where(strip == t * 4 + s, base + back + step * place, src)
+
+    row_ids = lax.broadcasted_iota(jnp.int32, (128, width), 0)
+
+    @pl.loop(0, 3 * width // 128)
+    def _(k):
+        hit = (row_ids + k * 128) == src
+        sel[pl.ds(pl.multiple_of(k * 128, 128), 128), :] = jnp.where(hit, 1.0, 0.0).astype(BF)
+
+    pair_first = (b - par) * per_dev
+    nrows = outo.shape[0]
+    picks = [jnp.int32(0)] * nrows
+    rank = jnp.int32(0)
+    for n in range(2 * per_dev):
+        sea = mask_s[pair_first + n]
+        for i in range(nrows):
+            picks[i] = jnp.where((sea == 1) & (rank == 2 * i + par), n, picks[i])
+        rank = rank + sea
+
+    for cp in edges:
+        cp.wait_recv()
+    rim = dot(ew[0], sel[:width]) + dot(ew[1], sel[width : 2 * width]) + dot(ew[2], sel[2 * width :])
+    rim = rim.astype(BF)
+    for i in range(nchan):
+        rl[i] = rim[:, i * 128 : i * 128 + 128]
+    rims = []
+    for d in range(1, nchan):
+        peer = lax.rem(c + d, nchan)
+        rims.append(remote(rl.at[peer], rg.at[c], (b, peer)))
+    for cp in rims:
+        cp.start()
+    own_rim = pltpu.make_async_copy(rl.at[c], rg.at[c], loc.at[9])
+    own_rim.start()
+
+    for cp in lcopies[3:6]:
+        cp.wait()
+    for cp in states:
+        cp.wait_recv()
+    own_rim.wait()
+    for cp in rims:
+        cp.wait_recv()
+
+    ring = jnp.concatenate(
+        [rg[i, :ach] for i in range(nchan)] + [rg[i, ach:] for i in range(nchan)], axis=0
+    )
+    for j in range(tp):
+        mine = jnp.where(lane128 // 64 == j, ring, jnp.zeros_like(ring))
+        rl_all = jnp.concatenate([xx[j], mine], axis=1)
+
+        @pl.loop(0, 9)
+        def _(tap):
+            xs[tap, :, j * PIX : (j + 1) * PIX] = dot(rl_all, sh[tap]).astype(BF)
+
+    forwards = []
+    for d in range(1, nchan):
+        origin = lax.rem(c + nchan - d, nchan)
+        ftaps = pl.ds(par * 5, 4)
+        forwards += [
+            remote(wa.at[ftaps, arow(origin), :], wa.at[ftaps, arow(origin), :], (sib, c)),
+            remote(wo.at[:, ohalf(origin, par), :], wo.at[:, ohalf(origin, par), :], (sib, c)),
+            remote(wc.at[ohalf(origin, par), :], wc.at[ohalf(origin, par), :], (sib, c)),
+        ]
+    for got, fwd in zip(weights, forwards):
+        got.wait_recv()
+        fwd.start()
+    for cp in lcopies[6:]:
+        cp.wait()
+    for cp in forwards:
+        cp.wait_recv()
+
+    dest = pl.ds(c * tp, tp)
+    finals = []
+    for j in range(tp):
+        acc = jnp.zeros((atot, PIX), F32)
+        for tap in range(9):
+            acc = acc + dot(wa[tap], xs[tap, :atot, j * PIX : (j + 1) * PIX])
+        an[j] = (xx[j, :atot].astype(F32) + gelu(acc)).astype(BF)
+    for d in range(1, nchan):
+        peer = lax.rem(c + d, nchan)
+        cp = remote(an.at[:, arow(peer), :], outa.at[dest], (b, peer))
+        cp.start()
+        finals.append(cp)
+    own_a = pltpu.make_async_copy(an.at[:, arow(c), :], outa.at[dest], loc.at[10])
+    own_a.start()
+    for j in range(tp):
+        acc = dot(wc[...], an[j])
+        for tap in range(9):
+            acc = acc + dot(wo[tap], xs[tap, atot:, j * PIX : (j + 1) * PIX])
+        on[j] = (xx[j, atot:].astype(F32) + gelu(acc)).astype(BF)
+    odest = pl.ds(par * per_dev + c * tp, tp)
+    for d in range(nchan):
+        peer = lax.rem(c + d, nchan)
+        for block in (b, sib) if d else (sib,):
+            cp = remote(on.at[:, orow(peer), :], og.at[odest], (block, peer))
+            cp.start()
+            finals.append(cp)
+    own_o = pltpu.make_async_copy(on.at[:, orow(c), :], og.at[odest], loc.at[11])
+    own_o.start()
+    own_a.wait()
+    own_o.wait()
+    for cp in finals:
+        cp.wait_recv()
+    for i in range(nrows):
+        outo[i] = og[picks[i]]
+    for cp in edges + states + weights + rims + forwards + finals:
+        cp.wait_send()
+
+
+def local_owner(
+    atmos_state, ocean_state, atmos_weight, ocean_weight, couple_weight, sea_mask, neighbours, rotations
+):
+    groups, nchan = lax.axis_size("tiles"), lax.axis_size("chan")
+    per_dev, ach, _ = atmos_state.shape
+    och = ocean_state.shape[1]
+    atot, otot, tp = ach * nchan, och * nchan, per_dev // nchan
+    rows, width = ach + och, per_dev * 64
+    copies = 2 + 11 * (nchan - 1) + 10 * (nchan - 1) + nchan + 6
+    anyspace = pl.BlockSpec(memory_space=pl.ANY)
+    smem = pl.BlockSpec(memory_space=pltpu.SMEM)
+    return pl.pallas_call(
+        functools.partial(owner_kernel, groups, nchan),
+        out_shape=(
+            jax.ShapeDtypeStruct(atmos_state.shape, BF),
+            jax.ShapeDtypeStruct((per_dev * 3 // 4, och, PIX), BF),
+        ),
+        in_specs=[anyspace] * 5 + [smem] * 3 + [anyspace] * 2,
+        out_specs=(anyspace, pl.BlockSpec(memory_space=pltpu.VMEM)),
+        scratch_shapes=[
+            pltpu.VMEM((per_dev, ach, PIX), BF),
+            pltpu.VMEM((per_dev, och, PIX), BF),
+            pltpu.VMEM((2, PIX, 128), BF),
+            pltpu.VMEM((9, PIX + 128, PIX), BF),
+            pltpu.VMEM((tp, atot + otot, PIX), BF),
+            pltpu.VMEM((3, rows, width), BF),
+            pltpu.VMEM((nchan, rows, 128), BF),
+            pltpu.VMEM((nchan, rows, 128), BF),
+            pltpu.VMEM((3 * width, width), BF),
+            pltpu.VMEM((9, atot, atot), BF),
+            pltpu.VMEM((9, otot, otot), BF),
+            pltpu.VMEM((otot, atot), BF),
+            pltpu.VMEM((9, atot + otot, tp * PIX), BF),
+            pltpu.VMEM((tp, atot, PIX), BF),
+            pltpu.VMEM((tp, otot, PIX), BF),
+            pltpu.VMEM((2 * per_dev, och, PIX), BF),
+            pltpu.SemaphoreType.DMA((12,)),
+            pltpu.SemaphoreType.DMA((copies,)),
+            pltpu.SemaphoreType.DMA((copies,)),
+        ],
+        compiler_params=pltpu.CompilerParams(
+            collective_id=0, has_side_effects=True, vmem_limit_bytes=40 * 2**20
+        ),
+        cost_estimate=pl.CostEstimate(flops=2 * 10**9, bytes_accessed=4 * 10**6, transcendentals=170000),
+    )(
+        atmos_state, ocean_state, atmos_weight, ocean_weight, couple_weight, sea_mask, neighbours, rotations,
+        jnp.asarray(edge_matrix(), BF), jnp.asarray(shift_matrix(), BF),
+    )
+
+
 def solution(mesh):
+    body = local_owner if mesh.shape["chan"] == 4 else local
     placed = (
         P("tiles", "chan", None),
         P("tiles", "chan", None),
@@ -194,7 +516,7 @@
         P(),
     )
     return jax.shard_map(
-        local,
+        body,
         mesh=mesh,
         in_specs=placed,
         out_specs=(P("tiles", "chan", None), P("tiles", "chan", None)),

time: 75.7 us -> 45.4 us (0.60)
  blocking collectives: 36.1 us -> 0 us
  Pallas kernels: 0 us -> 34.1 us
  matrix products: 8.62 us -> 0 us
  local copies, waits for them, and re-layouts: 17.3 us -> 10.3 us
  starting transfers between devices: 4.61 us -> 0 us
  other arithmetic: 3.81 us -> 0 us
  waiting for transfers between devices: 2.42 us -> 0 us
  between operations: 2.63 us -> 0.65 us
    all_gather x3 -> x0, blocking collectives: 36.1 us -> none  [the longest x1 15.2 us: local(): lax.all_gather(atmos_pad, 'chan', axis=1, tiled=True)]
    pallas_call x0 -> x1, Pallas kernels: none -> 34.1 us  [local_owner(): pl.pallas_call(functools.partial(owner_kernel, groups, nchan), out_shape=...]
    dot_general x19 -> x0, matrix products: 8.62 us -> none  [the longest x18 7.72 us: conv_step(): jnp.einsum('oc,bcp->bop', weight[tap_index], piece[:, :, offset:offset +...]
    unnamed x21 -> x20, local copies, waits for them, and re-layouts: 2.74 us -> 10.3 us
    ppermute x3 -> x0, starting transfers between devices: 4.61 us -> none  [the longest x1 4.53 us: padded_2(): lax.ppermute(head, axis, [((i + 1) % count, i) for i in range(count)])]
    gather x5 -> x0, local copies, waits for them, and re-layouts: 3.39 us -> none  [the longest x1 0.73 us: local(): received = partner(packed[send_tile], 'tiles', 0)]
    reshape x8 -> x0, local copies, waits for them, and re-layouts: 3.37 us -> none  [the longest x2 1.2 us: trim_columns(): accum.reshape(tile_count, chan_count, SIDE, SIDE + 2)[:, :, :, :SIDE]]
    ppermute x3 -> x0, waiting for transfers between devices: 2.42 us -> none  [the longest x1 2.42 us: padded_2(): lax.ppermute(tail, axis, [(i, (i + 1) % count) for i in range(count)])]
  transfers between devices with their start and end apart: 3 -> 0, of which waited for: 1 -> 0; matrix products, arithmetic and copies ran while one was open for 10% -> 0% of each run, Pallas kernels for 0% -> 0%
where the time goes in v1:
time: 45.4 us; the launch traced here: 45 us
  Pallas kernels  34.1 us (75%)
  local copies, waits for them, and re-layouts  10.3 us (23%)
  between operations  0.65 us (1%)
    pallas_call x1, Pallas kernels, local_owner(): pl.pallas_call(functools.partial(owner_kernel, groups, nchan), out_shape=...  34.1 us
    unnamed x20, local copies, waits for them, and re-layouts  10.3 us

profile of v1, /device:TPU:0, one launch (start us, length us, event | category | flops | bytes accessed | tf_op | source)
XLA Modules:
  0.0 45.0 jit_solution(15452641013765157393)
XLA Ops:
  0.6 0.8 %copy.12.nbr_s = s32[64,4]{1,0:T(8,128)S(1)} copy(s32[64,4]{0,1:T(4,128)} %param.16) | data formatting | bytes 2048 | tf_op args[6]
  1.4 0.8 %copy.13.rot_s = s32[64,4]{1,0:T(8,128)S(1)} copy(s32[64,4]{0,1:T(4,128)} %param.17) | data formatting | bytes 2048 | tf_op args[7]
  2.2 0.0 copy-start
  2.2 0.9 %copy-done = bf16[9,48,192]{2,1,0:T(8,128)(2,1)S(1)} copy-done((bf16[9,48,192]{2,1,0:T(8,128)(2,1)S(1)}, bf16[9,48,192]{2,1,0:T(8,128)(2,1)}, u32[]{:S(2)}) %copy-start) | copy-done | bytes 165912
  3.1 0.0 copy-start.1
  3.1 0.9 %copy-done.1 = bf16[8,48,256]{2,1,0:T(8,128)(2,1)S(1)} copy-done((bf16[8,48,256]{2,1,0:T(8,128)(2,1)S(1)}, bf16[8,48,256]{2,1,0:T(8,128)(2,1)}, u32[]{:S(2)}) %copy-start.1) | copy-done | bytes 196632
  4.0 0.0 copy-start.2
  4.0 0.9 %copy-done.2 = bf16[8,32,256]{2,1,0:T(8,128)(2,1)S(1)} copy-done((bf16[8,32,256]{2,1,0:T(8,128)(2,1)S(1)}, bf16[8,32,256]{2,1,0:T(8,128)(2,1)}, u32[]{:S(2)}) %copy-start.2) | copy-done | bytes 131096
  4.9 0.0 copy-start.3
  4.9 0.9 %copy-done.3 = bf16[9,32,128]{2,1,0:T(8,128)(2,1)S(1)} copy-done((bf16[9,32,128]{2,1,0:T(8,128)(2,1)S(1)}, bf16[9,32,128]{2,1,0:T(8,128)(2,1)}, u32[]{:S(2)}) %copy-start.3) | copy-done | bytes 73752
  5.8 0.0 copy-start.4
  5.8 0.7 %copy-done.4 = bf16[32,192]{1,0:T(8,128)(2,1)S(1)} copy-done((bf16[32,192]{1,0:T(8,128)(2,1)S(1)}, bf16[32,192]{1,0:T(8,128)(2,1)}, u32[]{:S(2)}) %copy-start.4) | copy-done | bytes 12312
  6.5 0.0 copy-start.5
  6.5 0.7 %copy-done.5 = s32[64]{0:T(128)S(1)} copy-done((s32[64]{0:T(128)S(1)}, s32[64]{0:T(128)}, u32[]{:S(2)}) %copy-start.5) | copy-done | bytes 280
  7.2 0.0 copy-start.6
  7.2 1.5 %copy-done.6 = bf16[9,384,256]{2,1,0:T(8,128)(2,1)S(1)} copy-done((bf16[9,384,256]{2,1,0:T(8,128)(2,1)S(1)}, bf16[9,384,256]{2,1,0:T(8,128)(2,1)}, u32[]{:S(2)}) %copy-start.6) | copy-done | bytes 1769496
  8.7 0.0 copy-start.7
  8.7 0.9 %copy-done.7 = bf16[2,256,128]{2,1,0:T(8,128)(2,1)S(1)} copy-done((bf16[2,256,128]{2,1,0:T(8,128)(2,1)S(1)}, bf16[2,256,128]{2,1,0:T(8,128)(2,1)}, u32[]{:S(2)}) %copy-start.7) | copy-done | bytes 131096
  9.6 34.1 %shard_map.113 = (bf16[8,48,256]{2,1,0:T(8,128)(2,1)S(1)}, bf16[6,32,256]{2,1,0:T(8,128)(2,1)S(1)}) custom-call(bf16[8,48,256]{2,1,0:T(8,128)(2,1)S(1)} %copy-done.1, bf16[8,32,256]{2,1,0:T(8,128)(2,1)S(1)} %copy-done.2, bf16[9,48,192]{2,1,0:T(8,128)(2,1)S(1)} %copy-done, bf16[9,32,128]{2,1,0:T(8,128)(2,1)S(1)} %copy-done.3, bf16[32,192]{1,0:T(8,128)(2,1)S(1)} %copy-done.4, ...), custom_call_target="tpu_custom_call" | custom-call | flops 2000000000 | bytes 4000000 | tf_op jit(solution)/shard_map/pallas_call | solution.py:467
  43.7 0.7 %copy.16 = bf16[8,48,256]{2,1,0:T(8,128)(2,1)} copy(bf16[8,48,256]{2,1,0:T(8,128)(2,1)S(1)} %get-tuple-element.4) | data formatting | bytes 393216
  44.3 0.6 %copy.17 = bf16[6,32,256]{2,1,0:T(8,128)(2,1)} copy(bf16[6,32,256]{2,1,0:T(8,128)(2,1)S(1)} %get-tuple-element.5) | data formatting | bytes 196608
Async XLA Ops:
  2.2 0.9 %copy-start = (bf16[9,48,192]{2,1,0:T(8,128)(2,1)S(1)}, bf16[9,48,192]{2,1,0:T(8,128)(2,1)}, u32[]{:S(2)}) copy-start(bf16[9,48,192]{2,1,0:T(8,128)(2,1)} %wa_hbm.1) | copy-start | bytes 497668
  3.1 0.9 %copy-start.1 = (bf16[8,48,256]{2,1,0:T(8,128)(2,1)S(1)}, bf16[8,48,256]{2,1,0:T(8,128)(2,1)}, u32[]{:S(2)}) copy-start(bf16[8,48,256]{2,1,0:T(8,128)(2,1)} %at_hbm.1) | copy-start | bytes 589828
  4.0 0.9 %copy-start.2 = (bf16[8,32,256]{2,1,0:T(8,128)(2,1)S(1)}, bf16[8,32,256]{2,1,0:T(8,128)(2,1)}, u32[]{:S(2)}) copy-start(bf16[8,32,256]{2,1,0:T(8,128)(2,1)} %oc_hbm.1) | copy-start | bytes 393220
  4.9 0.9 %copy-start.3 = (bf16[9,32,128]{2,1,0:T(8,128)(2,1)S(1)}, bf16[9,32,128]{2,1,0:T(8,128)(2,1)}, u32[]{:S(2)}) copy-start(bf16[9,32,128]{2,1,0:T(8,128)(2,1)} %wo_hbm.1) | copy-start | bytes 221188
  5.8 0.7 %copy-start.4 = (bf16[32,192]{1,0:T(8,128)(2,1)S(1)}, bf16[32,192]{1,0:T(8,128)(2,1)}, u32[]{:S(2)}) copy-start(bf16[32,192]{1,0:T(8,128)(2,1)} %wc_hbm.1) | copy-start | bytes 36868
  6.5 0.7 %copy-start.5 = (s32[64]{0:T(128)S(1)}, s32[64]{0:T(128)}, u32[]{:S(2)}) copy-start(s32[64]{0:T(128)} %mask_s.1) | copy-start | bytes 772
  7.2 1.5 %copy-start.6 = (bf16[9,384,256]{2,1,0:T(8,128)(2,1)S(1)}, bf16[9,384,256]{2,1,0:T(8,128)(2,1)}, u32[]{:S(2)}) copy-start(bf16[9,384,256]{2,1,0:T(8,128)(2,1)} %constant.5.clone.sh_hbm) | copy-start | bytes 5308420
  8.7 0.9 %copy-start.7 = (bf16[2,256,128]{2,1,0:T(8,128)(2,1)S(1)}, bf16[2,256,128]{2,1,0:T(8,128)(2,1)}, u32[]{:S(2)}) copy-start(bf16[2,256,128]{2,1,0:T(8,128)(2,1)} %constant.4.clone.ev_hbm) | copy-start | bytes 393220

commit v2 on v1

--- a/solution.py
+++ b/solution.py
@@ -231,14 +231,14 @@
 
 
 def owner_kernel(
-    groups, nchan, at_hbm, oc_hbm, wa_hbm, wo_hbm, wc_hbm, mask_s, nbr_s, rot_s, ev_hbm, sh_hbm,
+    groups, nchan, at_hbm, oc_hbm, wa_hbm, wo_hbm, wc_hbm, code_s, ev_hbm, sh_hbm,
     outa, outo,
-    at_v, oc_v, ev, sh, xx, ew, rl, rg, sel, wa, wo, wc, xs, an, on, og,
+    at_v, oc_v, ev, sh, xx, ew, rl, rg, sel, wa, wo, wc, xs, an, on, og, oacc,
     loc, ssem, rsem,
 ):
     per_dev, ach, _ = at_hbm.shape
     och = oc_hbm.shape[1]
-    atot = ach * nchan
+    atot, otot = ach * nchan, och * nchan
     tp = per_dev // nchan
     rows = ach + och
     b = lax.axis_index("tiles")
@@ -288,12 +288,13 @@
     for cp in lcopies[:3]:
         cp.wait()
 
-    first = b * per_dev
+    masks = per_dev * 4
+    here = masks + par * per_dev
     lane128 = lax.broadcasted_iota(jnp.int32, (1, 128), 1)
     for u in range(per_dev // 2):
         at_e = dot(at_v[2 * u], ev[0]) + dot(at_v[2 * u + 1], ev[1])
         oc_e = dot(oc_v[2 * u], ev[0]) + dot(oc_v[2 * u + 1], ev[1])
-        keep = jnp.where(lane128 < 64, mask_s[first + 2 * u], mask_s[first + 2 * u + 1])
+        keep = jnp.where(lane128 < 64, code_s[here + 2 * u], code_s[here + 2 * u + 1])
         ew[1, :ach, u * 128 : u * 128 + 128] = at_e.astype(BF)
         ew[1, ach:, u * 128 : u * 128 + 128] = jnp.where(keep > 0, oc_e, 0.0).astype(BF)
 
@@ -316,20 +317,22 @@
         peer = lax.rem(c + d, nchan)
         theirs = pl.ds(peer * tp, tp)
         states += [
-            remote(at_hbm.at[theirs], xx.at[:, arow(c), :], (b, peer)),
-            remote(oc_hbm.at[theirs], xx.at[:, xorow(c), :], (b, peer)),
+            remote(at_v.at[theirs], xx.at[:, arow(c), :], (b, peer)),
+            remote(oc_v.at[theirs], xx.at[:, xorow(c), :], (b, peer)),
         ]
     for cp in states:
         cp.start()
+    for cp in lcopies[6:]:
+        cp.wait()
+    taps = pl.ds(par * 4, 5)
+    big_weights = []
     for d in range(1, nchan):
         peer = lax.rem(c + d, nchan)
-        taps = pl.ds(par * 4, 5)
-        hrow = pl.ds(pl.multiple_of(par * half_o, 16), half_o)
         weights += [
-            remote(wa_hbm.at[taps], wa.at[taps, arow(c), :], (b, peer)),
-            remote(wo_hbm.at[:, hrow, :], wo.at[:, ohalf(c, par), :], (b, peer)),
-            remote(wc_hbm.at[hrow], wc.at[ohalf(c, par), :], (b, peer)),
+            remote(wo.at[:, ohalf(c, par), :], wo.at[:, ohalf(c, par), :], (b, peer)),
+            remote(wc.at[ohalf(c, par), :], wc.at[ohalf(c, par), :], (b, peer)),
         ]
+        big_weights.append(remote(wa.at[taps, arow(c), :], wa.at[taps, arow(c), :], (b, peer)))
     for cp in weights:
         cp.start()
 
@@ -339,12 +342,11 @@
     src = jnp.zeros((1, width), jnp.int32)
     for t in range(per_dev):
         for s in range(4):
-            nb = nbr_s[first + t, s]
-            rot = rot_s[first + t, s]
-            slot = lax.rem(lax.div(nb, per_dev) - b + 1 + groups, groups)
-            base = slot * width + lax.rem(nb, per_dev) * 64 + lax.rem(rot, 4) * SIDE
-            back = jnp.where(rot >= 4, SIDE - 1, 0)
-            step = jnp.where(rot >= 4, -1, 1)
+            code = code_s[s * per_dev + t]
+            turn = code & 7
+            back = jnp.where(turn >= 4, SIDE - 1, 0)
+            step = jnp.where(turn >= 4, -1, 1)
+            base = (code >> 3) * 64 + (turn & 3) * SIDE
             src = jnp.where(strip == t * 4 + s, base + back + step * place, src)
 
     row_ids = lax.broadcasted_iota(jnp.int32, (128, width), 0)
@@ -354,15 +356,18 @@
         hit = (row_ids + k * 128) == src
         sel[pl.ds(pl.multiple_of(k * 128, 128), 128), :] = jnp.where(hit, 1.0, 0.0).astype(BF)
 
-    pair_first = (b - par) * per_dev
     nrows = outo.shape[0]
     picks = [jnp.int32(0)] * nrows
     rank = jnp.int32(0)
+    own_rank = jnp.int32(0)
     for n in range(2 * per_dev):
-        sea = mask_s[pair_first + n]
+        sea = code_s[masks + n]
         for i in range(nrows):
             picks[i] = jnp.where((sea == 1) & (rank == 2 * i + par), n, picks[i])
+        own_rank = jnp.where(n == par * per_dev + c * tp, rank, own_rank)
         rank = rank + sea
+    own_sea = code_s[here + c * tp] == 1
+    takes_first = [own_sea & (own_rank % 2 == p) for p in range(2)]
 
     for cp in edges:
         cp.wait_recv()
@@ -374,11 +379,21 @@
     for d in range(1, nchan):
         peer = lax.rem(c + d, nchan)
         rims.append(remote(rl.at[peer], rg.at[c], (b, peer)))
-    for cp in rims:
+    for cp in rims + big_weights:
         cp.start()
     own_rim = pltpu.make_async_copy(rl.at[c], rg.at[c], loc.at[9])
     own_rim.start()
 
+    forwards = []
+    for d in range(1, nchan):
+        origin = lax.rem(c + nchan - d, nchan)
+        forwards += [
+            remote(wo.at[:, ohalf(origin, par), :], wo.at[:, ohalf(origin, par), :], (sib, c)),
+            remote(wc.at[ohalf(origin, par), :], wc.at[ohalf(origin, par), :], (sib, c)),
+        ]
+    for got, fwd in zip(weights, forwards):
+        got.wait_recv()
+        fwd.start()
     for cp in lcopies[3:6]:
         cp.wait()
     for cp in states:
@@ -390,29 +405,38 @@
     ring = jnp.concatenate(
         [rg[i, :ach] for i in range(nchan)] + [rg[i, ach:] for i in range(nchan)], axis=0
     )
+    parts = []
     for j in range(tp):
         mine = jnp.where(lane128 // 64 == j, ring, jnp.zeros_like(ring))
-        rl_all = jnp.concatenate([xx[j], mine], axis=1)
-
-        @pl.loop(0, 9)
-        def _(tap):
-            xs[tap, :, j * PIX : (j + 1) * PIX] = dot(rl_all, sh[tap]).astype(BF)
-
-    forwards = []
+        parts.append(jnp.concatenate([xx[j], mine], axis=1))
+
+    def shift(tap):
+        for j in range(tp):
+            xs[tap, :, j * PIX : (j + 1) * PIX] = dot(parts[j], sh[tap]).astype(BF)
+
+    pl.loop(0, 4)(shift)
+    pl.loop(5, 9)(shift)
+
+    def taken(tap, lo, hi, j):
+        return xx[j, lo:hi] if tap == 4 else xs[tap, lo:hi, j * PIX : (j + 1) * PIX]
+
+    for cp in forwards:
+        cp.wait_recv()
+    for j in range(tp):
+        acc = jnp.zeros((otot, PIX), F32)
+        for tap in range(9):
+            acc = acc + dot(wo[tap], taken(tap, atot, atot + otot, j))
+        oacc[j] = acc
+
+    big_forwards = []
     for d in range(1, nchan):
         origin = lax.rem(c + nchan - d, nchan)
         ftaps = pl.ds(par * 5, 4)
-        forwards += [
-            remote(wa.at[ftaps, arow(origin), :], wa.at[ftaps, arow(origin), :], (sib, c)),
-            remote(wo.at[:, ohalf(origin, par), :], wo.at[:, ohalf(origin, par), :], (sib, c)),
-            remote(wc.at[ohalf(origin, par), :], wc.at[ohalf(origin, par), :], (sib, c)),
-        ]
-    for got, fwd in zip(weights, forwards):
-        got.wait_recv()
+        fwd = remote(wa.at[ftaps, arow(origin), :], wa.at[ftaps, arow(origin), :], (sib, c))
+        big_weights[d - 1].wait_recv()
         fwd.start()
-    for cp in lcopies[6:]:
-        cp.wait()
-    for cp in forwards:
+        big_forwards.append(fwd)
+    for cp in big_forwards:
         cp.wait_recv()
 
     dest = pl.ds(c * tp, tp)
@@ -420,7 +444,7 @@
     for j in range(tp):
         acc = jnp.zeros((atot, PIX), F32)
         for tap in range(9):
-            acc = acc + dot(wa[tap], xs[tap, :atot, j * PIX : (j + 1) * PIX])
+            acc = acc + dot(wa[tap], taken(tap, 0, atot, j))
         an[j] = (xx[j, :atot].astype(F32) + gelu(acc)).astype(BF)
     for d in range(1, nchan):
         peer = lax.rem(c + d, nchan)
@@ -429,27 +453,28 @@
         finals.append(cp)
     own_a = pltpu.make_async_copy(an.at[:, arow(c), :], outa.at[dest], loc.at[10])
     own_a.start()
+    fresh = []
     for j in range(tp):
-        acc = dot(wc[...], an[j])
-        for tap in range(9):
-            acc = acc + dot(wo[tap], xs[tap, atot:, j * PIX : (j + 1) * PIX])
-        on[j] = (xx[j, atot:].astype(F32) + gelu(acc)).astype(BF)
-    odest = pl.ds(par * per_dev + c * tp, tp)
+        acc = oacc[j] + dot(wc[...], an[j])
+        fresh.append((xx[j, atot:].astype(F32) + gelu(acc)).astype(BF))
+    for p in range(2):
+        on[p] = jnp.where(takes_first[p], fresh[0], fresh[1])
+    slot = par * nchan + c
     for d in range(nchan):
         peer = lax.rem(c + d, nchan)
-        for block in (b, sib) if d else (sib,):
-            cp = remote(on.at[:, orow(peer), :], og.at[odest], (block, peer))
+        for block, p in ((b, par), (sib, 1 - par)) if d else ((sib, 1 - par),):
+            cp = remote(on.at[p, orow(peer), :], og.at[slot], (block, peer))
             cp.start()
             finals.append(cp)
-    own_o = pltpu.make_async_copy(on.at[:, orow(c), :], og.at[odest], loc.at[11])
+    own_o = pltpu.make_async_copy(on.at[par, orow(c), :], og.at[slot], loc.at[11])
     own_o.start()
     own_a.wait()
     own_o.wait()
     for cp in finals:
         cp.wait_recv()
     for i in range(nrows):
-        outo[i] = og[picks[i]]
-    for cp in edges + states + weights + rims + forwards + finals:
+        outo[i] = og[picks[i] >> 1]
+    for cp in edges + states + weights + big_weights + rims + forwards + big_forwards + finals:
         cp.wait_send()
 
 
@@ -462,6 +487,12 @@
     atot, otot, tp = ach * nchan, och * nchan, per_dev // nchan
     rows, width = ach + och, per_dev * 64
     copies = 2 + 11 * (nchan - 1) + 10 * (nchan - 1) + nchan + 6
+    group = lax.axis_index("tiles")
+    adjacent = lax.dynamic_slice_in_dim(neighbours, group * per_dev, per_dev, 0)
+    turns = lax.dynamic_slice_in_dim(rotations, group * per_dev, per_dev, 0)
+    near = (adjacent // per_dev - group + 1) % groups * per_dev + adjacent % per_dev
+    pair_mask = lax.dynamic_slice_in_dim(sea_mask, group // 2 * 2 * per_dev, 2 * per_dev, 0)
+    codes = jnp.concatenate([(near * 8 + turns).T.reshape(per_dev * 4), pair_mask])
     anyspace = pl.BlockSpec(memory_space=pl.ANY)
     smem = pl.BlockSpec(memory_space=pltpu.SMEM)
     return pl.pallas_call(
@@ -470,7 +501,7 @@
             jax.ShapeDtypeStruct(atmos_state.shape, BF),
             jax.ShapeDtypeStruct((per_dev * 3 // 4, och, PIX), BF),
         ),
-        in_specs=[anyspace] * 5 + [smem] * 3 + [anyspace] * 2,
+        in_specs=[anyspace] * 5 + [smem] + [anyspace] * 2,
         out_specs=(anyspace, pl.BlockSpec(memory_space=pltpu.VMEM)),
         scratch_shapes=[
             pltpu.VMEM((per_dev, ach, PIX), BF),
@@ -488,17 +519,18 @@
             pltpu.VMEM((9, atot + otot, tp * PIX), BF),
             pltpu.VMEM((tp, atot, PIX), BF),
             pltpu.VMEM((tp, otot, PIX), BF),
-            pltpu.VMEM((2 * per_dev, och, PIX), BF),
+            pltpu.VMEM((2 * nchan, och, PIX), BF),
+            pltpu.VMEM((tp, otot, PIX), F32),
             pltpu.SemaphoreType.DMA((12,)),
             pltpu.SemaphoreType.DMA((copies,)),
             pltpu.SemaphoreType.DMA((copies,)),
         ],
         compiler_params=pltpu.CompilerParams(
-            collective_id=0, has_side_effects=True, vmem_limit_bytes=40 * 2**20
+            collective_id=0, has_side_effects=True, vmem_limit_bytes=62 * 2**20
         ),
         cost_estimate=pl.CostEstimate(flops=2 * 10**9, bytes_accessed=4 * 10**6, transcendentals=170000),
     )(
-        atmos_state, ocean_state, atmos_weight, ocean_weight, couple_weight, sea_mask, neighbours, rotations,
+        atmos_state, ocean_state, atmos_weight, ocean_weight, couple_weight, codes,
         jnp.asarray(edge_matrix(), BF), jnp.asarray(shift_matrix(), BF),
     )
 

time: 45.4 us -> 34 us (0.75)
  local copies, waits for them, and re-layouts: 10.3 us -> 3.97 us
  Pallas kernels: 34.1 us -> 27.8 us
  other arithmetic: 0 us -> 1.38 us
    unnamed x20 -> x2, local copies, waits for them, and re-layouts: 10.3 us -> 3.16 us
    pallas_call x1, Pallas kernels: 34.1 us -> 27.8 us  [local_owner(): pl.pallas_call(functools.partial(owner_kernel, groups, nchan), out_shape=...]
    transpose x0 -> x1, other arithmetic: none -> 0.79 us  [local_owner(): (near * 8 + turns).T.reshape(per_dev * 4)]
    dynamic_slice x0 -> x1, local copies, waits for them, and re-layouts: none -> 0.73 us  [local_owner(): lax.dynamic_slice_in_dim(sea_mask, group // 2 * 2 * per_dev, 2 * per_dev, 0)]
    concatenate x0 -> x1, other arithmetic: none -> 0.59 us  [local_owner(): jnp.concatenate([(near * 8 + turns).T.reshape(per_dev * 4), pair_mask])]
where the time goes in v2:
time: 34 us; the launch traced here: 33.8 us
  Pallas kernels  27.8 us (82%)
  local copies, waits for them, and re-layouts  3.97 us (12%)
  other arithmetic  1.38 us (4%)
  between operations  0.66 us (2%)
    pallas_call x1, Pallas kernels, local_owner(): pl.pallas_call(functools.partial(owner_kernel, groups, nchan), out_shape=...  27.8 us
    unnamed x2, local copies, waits for them, and re-layouts  3.16 us
    transpose x1, other arithmetic, local_owner(): (near * 8 + turns).T.reshape(per_dev * 4)  0.79 us
    dynamic_slice x1, local copies, waits for them, and re-layouts, local_owner(): lax.dynamic_slice_in_dim(sea_mask, group // 2 * 2 * per_dev, 2 * per_dev, 0)  0.73 us

profile of v2, /device:TPU:0, one launch (start us, length us, event | category | flops | bytes accessed | tf_op | source)
XLA Modules:
  0.0 33.8 jit_solution(1484769709913392368)
XLA Ops:
  0.6 0.7 %dynamic_slice.11 = s32[16]{0:T(128)S(1)} dynamic-slice(s32[64]{0:T(128)} %param.15, s32[]{:T(128)S(6)} %select_n.32), dynamic_slice_sizes={16} | dynamic-slice | bytes 132 | tf_op jit(solution)/shard_map/dynamic_slice | solution.py:494
  1.4 0.8 %fusion.7 = s32[4,8]{1,0:T(4,128)S(1)} fusion(s32[64,4]{0,1:T(4,128)} %param.17, s32[]{:T(128)S(6)} %select_n.27, s32[64,4]{0,1:T(4,128)} %param.16, s32[]{:T(128)S(6)} %axis_index.15), kind=kLoop, calls=%fused_computation.15 | loop fusion | flops 1152 | bytes 392 | tf_op jit(solution)/shard_map/transpose | solution.py:495
  2.2 0.1 reshape.7
  2.3 0.6 %pad_add_fusion.code_s = s32[48]{0:T(128)} fusion(s32[16]{0:T(128)S(1)} %dynamic_slice.11, s32[32]{0:T(128)S(1)} %reshape.7), kind=kLoop, calls=%fused_computation.18 | loop fusion | flops 48 | bytes 384 | tf_op jit(solution)/shard_map/concatenate | solution.py:495
  2.8 27.8 %shard_map.113 = (bf16[8,48,256]{2,1,0:T(8,128)(2,1)}, bf16[6,32,256]{2,1,0:T(8,128)(2,1)}) custom-call(bf16[8,48,256]{2,1,0:T(8,128)(2,1)} %at_hbm.1, bf16[8,32,256]{2,1,0:T(8,128)(2,1)} %oc_hbm.1, bf16[9,48,192]{2,1,0:T(8,128)(2,1)} %wa_hbm.1, bf16[9,32,128]{2,1,0:T(8,128)(2,1)} %wo_hbm.1, bf16[32,192]{1,0:T(8,128)(2,1)} %wc_hbm.1, s32[48]{0:T(128)} %pad_add_fusion.code_s, ...), custom_call_target="tpu_custom_call" | custom-call | flops 2000000000 | bytes 4000000 | tf_op jit(solution)/shard_map/pallas_call | solution.py:498
  30.6 1.6 %copy.14 = bf16[8,48,256]{2,1,0:T(8,128)(2,1)} copy(bf16[8,48,256]{2,1,0:T(8,128)(2,1)} %get-tuple-element.4) | data formatting | bytes 393216
  32.3 1.5 %copy.15 = bf16[6,32,256]{2,1,0:T(8,128)(2,1)} copy(bf16[6,32,256]{2,1,0:T(8,128)(2,1)} %get-tuple-element.5) | data formatting | bytes 196608

commit v3 on v2

--- a/solution.py
+++ b/solution.py
@@ -222,6 +222,12 @@
     return out
 
 
+BLOCKS = (
+    [(t, None) for t in range(4)] + [(None, (0, 1)), (None, (2, 3)), (8, None)]
+    + [(t, None) for t in range(4, 8)] + [(None, (4, 5)), (None, (6, 7)), (None, (8, 8))]
+)
+
+
 def gelu(v):
     return 0.5 * v * (1.0 + jnp.tanh(np.float32(np.sqrt(2.0 / np.pi)) * (v + 0.044715 * (v * v * v))))
 
@@ -231,9 +237,9 @@
 
 
 def owner_kernel(
-    groups, nchan, at_hbm, oc_hbm, wa_hbm, wo_hbm, wc_hbm, code_s, ev_hbm, sh_hbm,
+    groups, nchan, at_hbm, oc_hbm, wa_hbm, wo_hbm, wc_hbm, mask_hbm, nbr_hbm, rot_hbm, ev_hbm, sh_hbm,
     outa, outo,
-    at_v, oc_v, ev, sh, xx, ew, rl, rg, sel, wa, wo, wc, xs, an, on, og, oacc,
+    at_v, oc_v, ev, sh, xx, ew, rl, rg, sel, wa, wo, wc, xs, an, on, og, oacc, wn, mask_s, nbr_s, rot_s,
     loc, ssem, rsem,
 ):
     per_dev, ach, _ = at_hbm.shape
@@ -278,23 +284,26 @@
         (at_hbm.at[own], xx.at[:, arow(c), :]),
         (oc_hbm.at[own], xx.at[:, xorow(c), :]),
         (sh_hbm, sh),
-        (wa_hbm, wa.at[:, arow(c), :]),
+        (wa_hbm, wn),
         (wo_hbm, wo.at[:, orow(c), :]),
         (wc_hbm, wc.at[orow(c), :]),
+        (mask_hbm, mask_s),
+        (nbr_hbm, nbr_s),
+        (rot_hbm, rot_s),
     ]
     lcopies = [pltpu.make_async_copy(s, t, loc.at[i]) for i, (s, t) in enumerate(locals_)]
     for cp in lcopies:
         cp.start()
-    for cp in lcopies[:3]:
+    for cp in lcopies[:3] + lcopies[9:]:
         cp.wait()
 
-    masks = per_dev * 4
-    here = masks + par * per_dev
+    first = b * per_dev
+    pair_first = (b - par) * per_dev
     lane128 = lax.broadcasted_iota(jnp.int32, (1, 128), 1)
     for u in range(per_dev // 2):
         at_e = dot(at_v[2 * u], ev[0]) + dot(at_v[2 * u + 1], ev[1])
         oc_e = dot(oc_v[2 * u], ev[0]) + dot(oc_v[2 * u + 1], ev[1])
-        keep = jnp.where(lane128 < 64, code_s[here + 2 * u], code_s[here + 2 * u + 1])
+        keep = jnp.where(lane128 < 64, mask_s[first + 2 * u], mask_s[first + 2 * u + 1])
         ew[1, :ach, u * 128 : u * 128 + 128] = at_e.astype(BF)
         ew[1, ach:, u * 128 : u * 128 + 128] = jnp.where(keep > 0, oc_e, 0.0).astype(BF)
 
@@ -322,9 +331,15 @@
         ]
     for cp in states:
         cp.start()
-    for cp in lcopies[6:]:
+    for cp in lcopies[6:9]:
         cp.wait()
-    taps = pl.ds(par * 4, 5)
+    for i, (lo, hi) in enumerate(BLOCKS):
+        if lo is not None:
+            block = wn[lo, :, :128]
+        else:
+            block = jnp.concatenate([wn[hi[0], :, 128:], wn[hi[1], :, 128:]], axis=1)
+        wa[i, arow(c), :] = block
+    taps = pl.ds(par * 7, 7)
     big_weights = []
     for d in range(1, nchan):
         peer = lax.rem(c + d, nchan)
@@ -342,11 +357,12 @@
     src = jnp.zeros((1, width), jnp.int32)
     for t in range(per_dev):
         for s in range(4):
-            code = code_s[s * per_dev + t]
-            turn = code & 7
+            near, turn = nbr_s[s, first + t], rot_s[s, first + t] & 7
+            slot = near // per_dev - b + 1
+            slot = jnp.where(slot < 0, slot + groups, jnp.where(slot >= groups, slot - groups, slot))
             back = jnp.where(turn >= 4, SIDE - 1, 0)
             step = jnp.where(turn >= 4, -1, 1)
-            base = (code >> 3) * 64 + (turn & 3) * SIDE
+            base = slot * width + near % per_dev * 64 + (turn & 3) * SIDE
             src = jnp.where(strip == t * 4 + s, base + back + step * place, src)
 
     row_ids = lax.broadcasted_iota(jnp.int32, (128, width), 0)
@@ -361,12 +377,12 @@
     rank = jnp.int32(0)
     own_rank = jnp.int32(0)
     for n in range(2 * per_dev):
-        sea = code_s[masks + n]
+        sea = mask_s[pair_first + n]
         for i in range(nrows):
             picks[i] = jnp.where((sea == 1) & (rank == 2 * i + par), n, picks[i])
         own_rank = jnp.where(n == par * per_dev + c * tp, rank, own_rank)
         rank = rank + sea
-    own_sea = code_s[here + c * tp] == 1
+    own_sea = mask_s[first + c * tp] == 1
     takes_first = [own_sea & (own_rank % 2 == p) for p in range(2)]
 
     for cp in edges:
@@ -381,7 +397,7 @@
         rims.append(remote(rl.at[peer], rg.at[c], (b, peer)))
     for cp in rims + big_weights:
         cp.start()
-    own_rim = pltpu.make_async_copy(rl.at[c], rg.at[c], loc.at[9])
+    own_rim = pltpu.make_async_copy(rl.at[c], rg.at[c], loc.at[12])
     own_rim.start()
 
     forwards = []
@@ -428,31 +444,49 @@
             acc = acc + dot(wo[tap], taken(tap, atot, atot + otot, j))
         oacc[j] = acc
 
+    def block_of(i, j):
+        lo, hi = BLOCKS[i]
+        if lo is not None:
+            return taken(lo, 0, 128, j)
+        last = taken(hi[1], 128, atot, j)
+        return jnp.concatenate(
+            [taken(hi[0], 128, atot, j), jnp.zeros_like(last) if hi[0] == hi[1] else last], axis=0
+        )
+
+    dest = pl.ds(c * tp, tp)
+    finals = []
+
+    def channels(owner):
+        for j in range(tp):
+            acc = jnp.zeros((ach, PIX), F32)
+            for i in range(0, 14, 2):
+                pair = jnp.concatenate([wa[i, arow(owner)], wa[i + 1, arow(owner)]], axis=1)
+                acc = acc + dot(pair, jnp.concatenate([block_of(i, j), block_of(i + 1, j)], axis=0))
+            an[j, arow(owner)] = (xx[j, arow(owner)].astype(F32) + gelu(acc)).astype(BF)
+
+    channels(c)
+    own_a = pltpu.make_async_copy(an.at[:, arow(c), :], outa.at[dest], loc.at[13])
+    own_a.start()
     big_forwards = []
-    for d in range(1, nchan):
+
+    def pass_on(d):
         origin = lax.rem(c + nchan - d, nchan)
-        ftaps = pl.ds(par * 5, 4)
-        fwd = remote(wa.at[ftaps, arow(origin), :], wa.at[ftaps, arow(origin), :], (sib, c))
+        blocks = wa.at[taps, arow(origin), :]
         big_weights[d - 1].wait_recv()
+        fwd = remote(blocks, blocks, (sib, c))
         fwd.start()
         big_forwards.append(fwd)
-    for cp in big_forwards:
-        cp.wait_recv()
-
-    dest = pl.ds(c * tp, tp)
-    finals = []
-    for j in range(tp):
-        acc = jnp.zeros((atot, PIX), F32)
-        for tap in range(9):
-            acc = acc + dot(wa[tap], taken(tap, 0, atot, j))
-        an[j] = (xx[j, :atot].astype(F32) + gelu(acc)).astype(BF)
+
+    pass_on(1)
     for d in range(1, nchan):
-        peer = lax.rem(c + d, nchan)
-        cp = remote(an.at[:, arow(peer), :], outa.at[dest], (b, peer))
+        if d + 1 < nchan:
+            pass_on(d + 1)
+        big_forwards[d - 1].wait_recv()
+        origin = lax.rem(c + nchan - d, nchan)
+        channels(origin)
+        cp = remote(an.at[:, arow(origin), :], outa.at[dest], (b, origin))
         cp.start()
         finals.append(cp)
-    own_a = pltpu.make_async_copy(an.at[:, arow(c), :], outa.at[dest], loc.at[10])
-    own_a.start()
     fresh = []
     for j in range(tp):
         acc = oacc[j] + dot(wc[...], an[j])
@@ -466,7 +500,7 @@
             cp = remote(on.at[p, orow(peer), :], og.at[slot], (block, peer))
             cp.start()
             finals.append(cp)
-    own_o = pltpu.make_async_copy(on.at[par, orow(c), :], og.at[slot], loc.at[11])
+    own_o = pltpu.make_async_copy(on.at[par, orow(c), :], og.at[slot], loc.at[14])
     own_o.start()
     own_a.wait()
     own_o.wait()
@@ -478,6 +512,14 @@
         cp.wait_send()
 
 
+def write_kernel(a, o, out_a, out_o, sem):
+    copies = [pltpu.make_async_copy(a, out_a, sem.at[0]), pltpu.make_async_copy(o, out_o, sem.at[1])]
+    for cp in copies:
+        cp.start()
+    for cp in copies:
+        cp.wait()
+
+
 def local_owner(
     atmos_state, ocean_state, atmos_weight, ocean_weight, couple_weight, sea_mask, neighbours, rotations
 ):
@@ -487,22 +529,16 @@
     atot, otot, tp = ach * nchan, och * nchan, per_dev // nchan
     rows, width = ach + och, per_dev * 64
     copies = 2 + 11 * (nchan - 1) + 10 * (nchan - 1) + nchan + 6
-    group = lax.axis_index("tiles")
-    adjacent = lax.dynamic_slice_in_dim(neighbours, group * per_dev, per_dev, 0)
-    turns = lax.dynamic_slice_in_dim(rotations, group * per_dev, per_dev, 0)
-    near = (adjacent // per_dev - group + 1) % groups * per_dev + adjacent % per_dev
-    pair_mask = lax.dynamic_slice_in_dim(sea_mask, group // 2 * 2 * per_dev, 2 * per_dev, 0)
-    codes = jnp.concatenate([(near * 8 + turns).T.reshape(per_dev * 4), pair_mask])
-    anyspace = pl.BlockSpec(memory_space=pl.ANY)
-    smem = pl.BlockSpec(memory_space=pltpu.SMEM)
-    return pl.pallas_call(
+    hbm = pl.BlockSpec(memory_space=pltpu.HBM)
+    vmem = pl.BlockSpec(memory_space=pltpu.VMEM)
+    kept = pl.pallas_call(
         functools.partial(owner_kernel, groups, nchan),
         out_shape=(
             jax.ShapeDtypeStruct(atmos_state.shape, BF),
             jax.ShapeDtypeStruct((per_dev * 3 // 4, och, PIX), BF),
         ),
-        in_specs=[anyspace] * 5 + [smem] + [anyspace] * 2,
-        out_specs=(anyspace, pl.BlockSpec(memory_space=pltpu.VMEM)),
+        in_specs=[hbm] * 10,
+        out_specs=(hbm, vmem),
         scratch_shapes=[
             pltpu.VMEM((per_dev, ach, PIX), BF),
             pltpu.VMEM((per_dev, och, PIX), BF),
@@ -513,7 +549,7 @@
             pltpu.VMEM((nchan, rows, 128), BF),
             pltpu.VMEM((nchan, rows, 128), BF),
             pltpu.VMEM((3 * width, width), BF),
-            pltpu.VMEM((9, atot, atot), BF),
+            pltpu.VMEM((14, atot, 128), BF),
             pltpu.VMEM((9, otot, otot), BF),
             pltpu.VMEM((otot, atot), BF),
             pltpu.VMEM((9, atot + otot, tp * PIX), BF),
@@ -521,18 +557,31 @@
             pltpu.VMEM((tp, otot, PIX), BF),
             pltpu.VMEM((2 * nchan, och, PIX), BF),
             pltpu.VMEM((tp, otot, PIX), F32),
-            pltpu.SemaphoreType.DMA((12,)),
+            pltpu.VMEM((9, ach, atot), BF),
+            pltpu.SMEM(sea_mask.shape, jnp.int32),
+            pltpu.SMEM(neighbours.shape[::-1], jnp.int32),
+            pltpu.SMEM(rotations.shape[::-1], jnp.int32),
+            pltpu.SemaphoreType.DMA((16,)),
             pltpu.SemaphoreType.DMA((copies,)),
             pltpu.SemaphoreType.DMA((copies,)),
         ],
         compiler_params=pltpu.CompilerParams(
-            collective_id=0, has_side_effects=True, vmem_limit_bytes=62 * 2**20
+            collective_id=0, has_side_effects=True, vmem_limit_bytes=63 * 2**20 + 2**19
         ),
         cost_estimate=pl.CostEstimate(flops=2 * 10**9, bytes_accessed=4 * 10**6, transcendentals=170000),
     )(
-        atmos_state, ocean_state, atmos_weight, ocean_weight, couple_weight, codes,
+        atmos_state, ocean_state, atmos_weight, ocean_weight, couple_weight, sea_mask, neighbours.T, rotations.T,
         jnp.asarray(edge_matrix(), BF), jnp.asarray(shift_matrix(), BF),
     )
+    anyspace = pl.BlockSpec(memory_space=pl.ANY)
+    return pl.pallas_call(
+        write_kernel,
+        out_shape=tuple(jax.ShapeDtypeStruct(k.shape, BF) for k in kept),
+        in_specs=[anyspace] * 2,
+        out_specs=(hbm, hbm),
+        scratch_shapes=[pltpu.SemaphoreType.DMA((2,))],
+        compiler_params=pltpu.CompilerParams(vmem_limit_bytes=63 * 2**20 + 2**19),
+    )(*kept)
 
 
 def solution(mesh):

time: 34 us -> 37.6 us (1.11)
  Pallas kernels: 27.8 us -> 36.8 us
  local copies, waits for them, and re-layouts: 3.97 us -> 0 us
  other arithmetic: 1.38 us -> 0 us
    pallas_call x0 -> x1, Pallas kernels: none -> 10.1 us  [local_owner(): pl.pallas_call(write_kernel, out_shape=tuple((jax.ShapeDtypeStruct(k.shap...]
    unnamed x2 -> x0, local copies, waits for them, and re-layouts: 3.16 us -> none
    pallas_call x1, Pallas kernels: 27.8 us -> 26.8 us  [local_owner(): pl.pallas_call(functools.partial(owner_kernel, groups, nchan), out_shape=...]
    transpose x1 -> x0, other arithmetic: 0.79 us -> none  [local_owner(): (near * 8 + turns).T.reshape(per_dev * 4)]
    dynamic_slice x1 -> x0, local copies, waits for them, and re-layouts: 0.73 us -> none  [local_owner(): lax.dynamic_slice_in_dim(sea_mask, group // 2 * 2 * per_dev, 2 * per_dev, 0)]
    concatenate x1 -> x0, other arithmetic: 0.59 us -> none  [local_owner(): jnp.concatenate([(near * 8 + turns).T.reshape(per_dev * 4), pair_mask])]
where the time goes in v3:
time: 37.6 us; the launch traced here: 37.5 us
  Pallas kernels  36.8 us (98%)
  between operations  0.64 us (2%)
    pallas_call x1, Pallas kernels, local_owner(): pl.pallas_call(functools.partial(owner_kernel, groups, nchan), out_shape=...  26.8 us
    pallas_call x1, Pallas kernels, local_owner(): pl.pallas_call(write_kernel, out_shape=tuple((jax.ShapeDtypeStruct(k.shap...  10.1 us

profile of v3, /device:TPU:0, one launch (start us, length us, event | category | flops | bytes accessed | tf_op | source)
XLA Modules:
  0.0 37.5 jit_solution(6147437374222078071)
XLA Ops:
  0.6 26.8 %shard_map.113 = (bf16[8,48,256]{2,1,0:T(8,128)(2,1)}, bf16[6,32,256]{2,1,0:T(8,128)(2,1)}) custom-call(bf16[8,48,256]{2,1,0:T(8,128)(2,1)} %at_hbm.1, bf16[8,32,256]{2,1,0:T(8,128)(2,1)} %oc_hbm.1, bf16[9,48,192]{2,1,0:T(8,128)(2,1)} %wa_hbm.1, bf16[9,32,128]{2,1,0:T(8,128)(2,1)} %wo_hbm.1, bf16[32,192]{1,0:T(8,128)(2,1)} %wc_hbm.1, s32[64]{0:T(128)} %mask_hbm.1, ...), custom_call_target="tpu_custom_call" | custom-call | flops 2000000000 | bytes 4000000 | tf_op jit(solution)/shard_map/pallas_call | solution.py:534
  27.4 10.1 %shard_map.114 = (bf16[8,48,256]{2,1,0:T(8,128)(2,1)}, bf16[6,32,256]{2,1,0:T(8,128)(2,1)}) custom-call(bf16[8,48,256]{2,1,0:T(8,128)(2,1)} %get-tuple-element.4.a, bf16[6,32,256]{2,1,0:T(8,128)(2,1)} %get-tuple-element.5.o), custom_call_target="tpu_custom_call" | custom-call | tf_op jit(solution)/shard_map/pallas_call | solution.py:577

commit v4 on v3

--- a/solution.py
+++ b/solution.py
@@ -512,12 +512,9 @@
         cp.wait_send()
 
 
-def write_kernel(a, o, out_a, out_o, sem):
-    copies = [pltpu.make_async_copy(a, out_a, sem.at[0]), pltpu.make_async_copy(o, out_o, sem.at[1])]
-    for cp in copies:
-        cp.start()
-    for cp in copies:
-        cp.wait()
+def write_kernel(a, o, out_a, out_o):
+    out_a[...] = a[...]
+    out_o[...] = o[...]
 
 
 def local_owner(
@@ -573,13 +570,11 @@
         atmos_state, ocean_state, atmos_weight, ocean_weight, couple_weight, sea_mask, neighbours.T, rotations.T,
         jnp.asarray(edge_matrix(), BF), jnp.asarray(shift_matrix(), BF),
     )
-    anyspace = pl.BlockSpec(memory_space=pl.ANY)
     return pl.pallas_call(
         write_kernel,
         out_shape=tuple(jax.ShapeDtypeStruct(k.shape, BF) for k in kept),
-        in_specs=[anyspace] * 2,
-        out_specs=(hbm, hbm),
-        scratch_shapes=[pltpu.SemaphoreType.DMA((2,))],
+        in_specs=[vmem] * 2,
+        out_specs=(vmem, vmem),
         compiler_params=pltpu.CompilerParams(vmem_limit_bytes=63 * 2**20 + 2**19),
     )(*kept)
 

time: 37.6 us -> 29.3 us (0.78)
  Pallas kernels: 36.8 us -> 28.5 us
    pallas_call x1, Pallas kernels: 10.1 us -> 1.71 us  [local_owner(): pl.pallas_call(write_kernel, out_shape=tuple((jax.ShapeDtypeStruct(k.shap...]
where the time goes in v4:
time: 29.3 us; the launch traced here: 29.1 us
  Pallas kernels  28.5 us (97%)
  between operations  0.64 us (2%)
    pallas_call x1, Pallas kernels, local_owner(): pl.pallas_call(functools.partial(owner_kernel, groups, nchan), out_shape=...  26.8 us
    pallas_call x1, Pallas kernels, local_owner(): pl.pallas_call(write_kernel, out_shape=tuple((jax.ShapeDtypeStruct(k.shap...  1.71 us

profile of v4, /device:TPU:0, one launch (start us, length us, event | category | flops | bytes accessed | tf_op | source)
XLA Modules:
  0.0 29.1 jit_solution(11640620278680175846)
XLA Ops:
  0.6 26.8 %shard_map.113 = (bf16[8,48,256]{2,1,0:T(8,128)(2,1)}, bf16[6,32,256]{2,1,0:T(8,128)(2,1)}) custom-call(bf16[8,48,256]{2,1,0:T(8,128)(2,1)} %at_hbm.1, bf16[8,32,256]{2,1,0:T(8,128)(2,1)} %oc_hbm.1, bf16[9,48,192]{2,1,0:T(8,128)(2,1)} %wa_hbm.1, bf16[9,32,128]{2,1,0:T(8,128)(2,1)} %wo_hbm.1, bf16[32,192]{1,0:T(8,128)(2,1)} %wc_hbm.1, s32[64]{0:T(128)} %mask_hbm.1, ...), custom_call_target="tpu_custom_call" | custom-call | flops 2000000000 | bytes 4000000 | tf_op jit(solution)/shard_map/pallas_call | solution.py:531
  27.4 1.7 %shard_map.114 = (bf16[8,48,256]{2,1,0:T(8,128)(2,1)}, bf16[6,32,256]{2,1,0:T(8,128)(2,1)}) custom-call(bf16[8,48,256]{2,1,0:T(8,128)(2,1)} %get-tuple-element.4.a, bf16[6,32,256]{2,1,0:T(8,128)(2,1)} %get-tuple-element.5.o), custom_call_target="tpu_custom_call" | custom-call | tf_op jit(solution)/shard_map/pallas_call | solution.py:573
